TPU v7x, 256 devices: a whole 4x4x8 slice. The times are simulated.
256 devices in a mesh: ctx: 32 (over z, x), dp: 8 (over y, core).
Axes of the slice: x: 4, y: 4, z: 8, core: 2. Of those that a mesh axis runs over, the one named last changes fastest.
Arguments:
- mel_frames: bfloat16 [8, 4096, 128], P('dp', 'ctx'), may hold values from -6 to 6
- conv_weight: bfloat16 [384, 1280], replicated, may hold values from -0.3125 to 0.3125
- conv_bias: float32 [1280], replicated, may hold values from -3 to 3
- video_hidden: bfloat16 [8, 4096, 5120], P('dp', 'ctx'), may hold values from -6 to 6
- video_count: int32 [8, 32], P('dp', 'ctx'), may hold values from 0 to 128, as said below
- video_places: int32 [8, 4096], P('dp', 'ctx'), may hold values from 0 to 6143, as said below
- audio_places: int32 [8, 4096], P('dp', 'ctx'), may hold values from 0 to 6143, as said below
- cotangent: bfloat16 [8, 6144, 3584], P('dp', 'ctx'), may hold values from -0.049804688 to 0.049804688
Outputs:
- grad_merger: float32 [32, 640, 896], P('ctx', 'dp')
- grad_audio: float32 [32, 160, 896], P('ctx', 'dp')
Inputs may be any that keep to these rules, and one draw needn't show every extreme that they name: `video_count`: in every sequence, shards 2i and 2i + 1 of encoder time hold 128 live video rows together, and some shard holds 128. `video_places`: in each sequence the live video slots (slot index within its shard below the shard's count) and the audio rows name every position exactly once; slots at or past the count hold arbitrary positions. `audio_places`: see video_places.
All inputs are finite; a program needn't handle non-finite values.
Results may differ from a plain program's by a relative error of at most 0.0029.
Values may be sent and summed in bfloat16 or wider, within the bound.
A program may use at most 128 MiB of HBM per device.

v0:
```python
import jax
import jax.numpy as jnp
from jax import lax
from jax.sharding import Mesh, PartitionSpec as P

GRID_ROWS = 8
GRID_COLS = 4


def local(
    mel, conv_weight, conv_bias, video_hidden, video_count, video_places, audio_places, cotangent
):
    z = lax.axis_index("z")
    hidden = video_hidden[0]
    places = video_places[0]
    upstream = cotangent[0]
    block_cols = upstream.shape[1] // GRID_COLS
    enc = conv_weight.shape[1] // GRID_ROWS
    cols = lax.all_to_all(
        jnp.transpose(upstream.reshape(-1, GRID_COLS, block_cols), (1, 0, 2)), "x", 0, 0, tiled=True
    )
    up = lax.all_gather(cols, "z", tiled=True).reshape(-1, block_cols)
    live_count = video_count[0, 0]
    middle = hidden.shape[0] // 2
    pairs = [(i, i ^ 1) for i in range(lax.axis_size("x"))]
    got_rows, got_places = lax.ppermute((hidden[middle:], places[middle:]), "x", pairs)
    joined = jnp.concatenate([hidden[:middle], got_rows], axis=0)
    joined_places = jnp.concatenate([places[:middle], got_places], axis=0)
    ids = jnp.arange(middle, dtype=jnp.int32)
    source = jnp.where((ids < live_count) | (live_count >= middle), ids, middle + ids - live_count)
    rows = jnp.take(joined, source, axis=0)
    spots = jnp.take(joined_places, source, axis=0)
    rows = lax.all_to_all(
        jnp.transpose(rows.reshape(middle, GRID_ROWS, -1), (1, 0, 2)), "z", 0, 0, tiled=True
    )
    rows = lax.all_gather(rows, "x", axis=1, tiled=False)
    rows = rows.reshape(-1, rows.shape[-1])
    spots = lax.all_gather(lax.all_gather(spots, "x"), "z").reshape(-1)
    frames = lax.all_gather(lax.all_gather(mel[0], "x"), "z").reshape(-1, mel.shape[-1])
    audio_spots = lax.all_gather(lax.all_gather(audio_places[0], "x"), "z").reshape(-1)
    pad = jnp.zeros((1, frames.shape[1]), frames.dtype)
    padded = jnp.concatenate([pad, frames, pad], axis=0)
    windows = jnp.concatenate([padded[:-2], padded[1:-1], padded[2:]], axis=1)
    weight = lax.dynamic_slice_in_dim(conv_weight, z * enc, enc, axis=1)
    bias = lax.dynamic_slice_in_dim(conv_bias, z * enc, enc, axis=0)
    conv = jnp.dot(windows, weight, preferred_element_type=jnp.float32) + bias
    audio = jax.nn.gelu(conv, approximate=False).astype(jnp.bfloat16)
    contract = (((0,), (0,)), ((), ()))
    merger = lax.dot_general(
        rows, jnp.take(up, spots, axis=0), contract, preferred_element_type=jnp.float32
    )
    audio_block = lax.dot_general(
        audio, jnp.take(up, audio_spots, axis=0), contract, preferred_element_type=jnp.float32
    )
    merger = lax.psum_scatter(merger, ("y", "core"), tiled=True)
    audio_block = lax.psum_scatter(
        audio_block.reshape(GRID_ROWS, enc // GRID_ROWS, block_cols), ("y", "core"), tiled=True
    )
    return (merger[None], audio_block)


def solution(mesh):
    whole = Mesh(mesh.devices.reshape(8, 4, 4, 2), ("z", "x", "y", "core"))
    dp, ctx = (("y", "core"), ("z", "x"))
    return jax.shard_map(
        local,
        mesh=whole,
        in_specs=(
            P(dp, ctx, None),
            P(),
            P(),
            P(dp, ctx, None),
            P(dp, ctx),
            P(dp, ctx),
            P(dp, ctx),
            P(dp, ctx, None),
        ),
        out_specs=(P(ctx, dp, None), P(ctx, dp, None)),
        check_vma=False,
    )
```

profile of v0, /device:TPU:2, one launch (start us, length us, event | category | flops | bytes accessed | tf_op | source)
XLA Modules:
  0.0 306.2 jit_solution(9559356676186818272)
XLA Ops:
  7.2 0.0 copy-start
  7.2 0.0 all-gather.16.cloned.1.call-start
  7.2 13.5 %all_gather.43 = bf16[4,128,128]{2,1,0:T(8,128)(2,1)} all-gather(bf16[1,128,128]{2,1,0:T(8,128)(2,1)} %param.8), channel_id=1, replica_groups=mesh['z'=8,'x'=4,'y'=4,'core'=2] {'x'}, dimensions={0}, use_global_device_ids=true | all-gather | bytes 163840 | tf_op jit(solution)/shard_map/all_gather | solution.py:39
  20.7 0.0 all-gather.16.cloned.1.call-update
  20.7 0.0 all-gather.12.cloned.1.call-start
  20.8 2.8 reshape_squeeze.3
  23.6 0.2 copy.21
  23.7 0.0 copy-start.2
  23.7 20.1 %all_to_all.10 = bf16[4,192,896]{2,1,0:T(8,128)(2,1)} all-to-all(bf16[4,192,896]{2,1,0:T(8,128)(2,1)S(1)} %copy.21), channel_id=1, replica_groups=mesh['z'=8,'x'=4,'y'=4,'core'=2] {'x'}, dimensions={0} | all-to-all | bytes 2752512 | tf_op jit(solution)/shard_map/all_to_all | solution.py:19
  43.8 0.0 all-gather.12.cloned.1.call-update
  43.9 1.0 slice_bitcast_fusion.1
  44.8 0.6 collective-permute-start
  46.1 9.9 %collective-permute-done = bf16[64,5120]{1,0:T(8,128)(2,1)S(1)} collective-permute-done((bf16[64,5120]{1,0:T(8,128)(2,1)}, bf16[64,5120]{1,0:T(8,128)(2,1)S(1)}, u32[]{:S(2)}, u32[]{:S(2)}) %collective-permute-start) | collective-permute-done | bytes 655392 | tf_op jit(solution)/shard_map/ppermute | solution.py:26
  56.1 0.9 copy-done.4
  56.9 1.2 pad_maximum_fusion
  58.1 0.9 gather_fusion
  59.0 0.0 copy-start.5
  59.1 0.0 copy-start.6
  59.1 1.0 fusion.58
  60.1 9.3 %all-to-all-start = ((bf16[8,64,640]{2,1,0:T(8,128)(2,1)}), bf16[8,64,640]{2,1,0:T(8,128)(2,1)S(1)}, u32[]{:S(2)}, u32[]{:S(2)}) async-start(bf16[8,64,640]{2,1,0:T(8,128)(2,1)} %fusion.58), calls=%async_computation | async-start | bytes 1310720 | tf_op jit(solution)/shard_map/all_to_all | solution.py:33
  69.4 0.0 all-gather.14.cloned.1.call-start
  69.5 0.1 slice_bitcast_fusion.3
  69.6 1.5 collective-permute-start.1
  71.1 7.5 %all-gather.6 = s32[4,1,128]{2,1,0:T(1,128)S(1)} all-gather(s32[1,1,128]{2,1,0:T(1,128)S(1)} %bitcast.54), channel_id=1, replica_groups=mesh['z'=8,'x'=4,'y'=4,'core'=2] {'x'}, dimensions={0}, use_global_device_ids=true | all-gather | bytes 2560 | tf_op jit(solution)/shard_map/all_gather | solution.py:40
  78.5 25.6 %all-gather.7 = s32[8,4,128]{2,1,0:T(4,128)S(1)} all-gather(s32[1,4,128]{2,1,0:T(4,128)S(1)} %bitcast.53), channel_id=5, replica_groups=mesh['z'=8,'x'=4,'y'=4,'core'=2] {'z'}, dimensions={0}, use_global_device_ids=true | all-gather | bytes 18432 | tf_op jit(solution)/shard_map/all_gather | solution.py:40
  104.2 0.9 copy-done.1
  105.0 0.0 all-gather.14.cloned.1.call-update
  105.1 0.0 reduce-scatter.7.cloned.1.call-start
  105.2 0.8 dynamic_slice.7
  106.0 0.1 pad_add_fusion
  106.0 0.8 gather_fusion.1
  106.8 8.8 %all-gather.4 = s32[4,1,64]{2,1,0:T(1,128)S(1)} all-gather(s32[1,1,64]{2,1,0:T(1,128)S(1)} %fusion.62), channel_id=1, replica_groups=mesh['z'=8,'x'=4,'y'=4,'core'=2] {'x'}, dimensions={0}, use_global_device_ids=true | all-gather | bytes 1280 | tf_op jit(solution)/shard_map/all_gather | solution.py:38
  115.6 21.3 %all-gather.5 = s32[8,4,64]{2,1,0:T(4,128)S(1)} all-gather(s32[1,4,64]{2,1,0:T(4,128)S(1)} %bitcast.52), channel_id=3, replica_groups=mesh['z'=8,'x'=4,'y'=4,'core'=2] {'z'}, dimensions={0}, use_global_device_ids=true | all-gather | bytes 9216 | tf_op jit(solution)/shard_map/all_gather | solution.py:38
  136.9 0.1 reshape.197
  137.0 3.1 %pad_slice_fusion.1 = (bf16[4096,128]{1,0:T(8,128)(2,1)S(1)}, bf16[4096,128]{1,0:T(8,128)(2,1)}) fusion(bf16[4096,128]{1,0:T(8,128)(2,1)} %bitcast.46), kind=kLoop, calls=%fused_computation.69 | loop fusion | bytes 3145728 | tf_op jit(solution)/shard_map/slice | solution.py:43
  140.1 47.5 %all-gather.12.cloned.1.call-done = bf16[32,192,896]{2,1,0:T(8,128)(2,1)} async-done(((bf16[4,192,896]{2,1,0:T(8,128)(2,1)}), bf16[32,192,896]{2,1,0:T(8,128)(2,1)}) %all-gather.12.cloned.1.call-update) | async-done | bytes 11010064 | tf_op jit(solution)/shard_map/all_gather | solution.py:22
  187.7 25.4 %gather_fusion.3 = bf16[4096,896]{1,0:T(8,128)(2,1)} fusion(bf16[6144,896]{1,0:T(8,128)(2,1)} %bitcast.42, s32[4096]{0:T(1024)S(1)} %broadcast_clamp_fusion), kind=kCustom, calls=%fused_computation.3 | custom fusion | bytes 14696448 | tf_op jit(solution)/shard_map/jit(_take)/gather | solution.py:53
  213.1 13.1 %fusion = f32[160,896]{1,0:T(8,128)} fusion(bf16[4096,896]{1,0:T(8,128)(2,1)} %gather_fusion.3, pred[4096]{0:T(1024)(128)(4,1)S(1)} %compare_and_fusion, bf16[4096,128]{1,0:T(8,128)(2,1)} %get-tuple-element.13, bf16[4096,128]{1,0:T(8,128)(2,1)S(1)} %bitcast.47, bf16[4096,128]{1,0:T(8,128)(2,1)S(1)} %get-tuple-element.12, f32[160]{0:T(256)S(1)} %dynamic_slice.7, ...), kind=kOutput, calls=%fused_computation.4 | convolution fusion | flops 1734082560 | bytes 11260932 | tf_op jit(solution)/shard_map/dot_general | solution.py:52
  226.3 2.0 reshape.201
  228.2 0.0 reduce-scatter.7.cloned.1.call-update
  228.3 0.3 reduce-scatter.5.cloned.1.call-start
  228.6 0.1 reshape.195
  228.7 16.0 %gather_fusion.2 = bf16[2048,896]{1,0:T(8,128)(2,1)} fusion(bf16[6144,896]{1,0:T(8,128)(2,1)} %bitcast.43, s32[2048]{0:T(1024)S(1)} %broadcast_clamp_fusion.1), kind=kCustom, calls=%fused_computation.2 | custom fusion | bytes 7348224 | tf_op jit(solution)/shard_map/jit(_take)/gather | solution.py:50
  244.7 7.2 %fusion.4 = f32[640,896]{1,0:T(8,128)} fusion(bf16[2048,640]{1,0:T(8,128)(2,1)} %bitcast.55, bf16[2048,896]{1,0:T(8,128)(2,1)} %gather_fusion.2, pred[2048]{0:T(1024)(128)(4,1)S(1)} %compare_and_fusion.1), kind=kOutput, calls=%fused_computation.10 | convolution fusion | flops 2350645248 | bytes 8587264 | tf_op jit(solution)/shard_map/dot_general | solution.py:49
  251.9 0.0 reduce-scatter.5.cloned.1.call-update
  251.9 9.3 %reduce-scatter.7.cloned.1.call-done = f32[1,20,896]{2,1,0:T(8,128)} async-done(((f32[8,20,896]{2,1,0:T(8,128)}), f32[1,20,896]{2,1,0:T(8,128)}) %reduce-scatter.7.cloned.1.call-update) | async-done | bytes 71696
  261.2 1.6 copy.22
  262.8 36.9 %reduce-scatter.5.cloned.1.call-done = f32[80,896]{1,0:T(8,128)} async-done(((f32[640,896]{1,0:T(8,128)}), f32[80,896]{1,0:T(8,128)}) %reduce-scatter.5.cloned.1.call-update) | async-done | bytes 286736 | tf_op jit(solution)/shard_map/reduce_scatter | solution.py:55
  (22 shorter events, 0.1 us)
Async XLA Ops:
  7.2 206.0 %copy-start = (bf16[384,1280]{1,0:T(8,128)(2,1)S(1)}, bf16[384,1280]{1,0:T(8,128)(2,1)}, u32[]{:S(2)}) copy-start(bf16[384,1280]{1,0:T(8,128)(2,1)} %param.9) | copy-start | bytes 2949124
  7.2 129.9 %all-gather.16.cloned.1.call-start = ((), (), s32[]{:S(2)}) async-start(), calls=%async_computation.7 | async-start | bytes 1179648 | tf_op jit(solution)/shard_map/all_gather | solution.py:39
  20.7 166.9 %all-gather.12.cloned.1.call-start = ((), (), s32[]{:S(2)}) async-start(), calls=%async_computation.4 | async-start | bytes 12386304 | tf_op jit(solution)/shard_map/all_gather | solution.py:22
  23.7 20.1 %copy-start.2 = (bf16[1,128,5120]{2,1,0:T(8,128)(2,1)S(1)}, bf16[1,128,5120]{2,1,0:T(8,128)(2,1)}, u32[]{:S(2)}) copy-start(bf16[1,128,5120]{2,1,0:T(8,128)(2,1)} %param.11) | copy-start | bytes 3932164
  44.8 11.2 %collective-permute-start = (bf16[64,5120]{1,0:T(8,128)(2,1)}, bf16[64,5120]{1,0:T(8,128)(2,1)S(1)}, u32[]{:S(2)}, u32[]{:S(2)}) collective-permute-start(bf16[64,5120]{1,0:T(8,128)(2,1)} %get-tuple-element.11), channel_id=1, source_target_pairs={{0,8},{8,0},{16,24},{24,16},{1,9},{9,1},{17,25},{25,17},{2,10},{10... | collective-permute-start | bytes 1966088 | tf_op jit(solution)/shard_map/ppermute | solution.py:26
  56.0 0.9 copy-start.4
  59.0 10.4 %copy-start.5 = (s32[1,128]{1,0:T(1,128)S(1)}, s32[1,128]{1,0:T(1,128)}, u32[]{:S(2)}) copy-start(s32[1,128]{1,0:T(1,128)} %param.13) | copy-start | bytes 1540
  59.1 12.0 %copy-start.6 = (s32[1,128]{1,0:T(1,128)S(1)}, s32[1,128]{1,0:T(1,128)}, u32[]{:S(2)}) copy-start(s32[1,128]{1,0:T(1,128)} %param.14) | copy-start | bytes 1540
  60.1 44.1 %all-to-all-start = ((bf16[8,64,640]{2,1,0:T(8,128)(2,1)}), bf16[8,64,640]{2,1,0:T(8,128)(2,1)S(1)}, u32[]{:S(2)}, u32[]{:S(2)}) async-start(bf16[8,64,640]{2,1,0:T(8,128)(2,1)} %fusion.58), calls=%async_computation | async-start | bytes 1310720 | tf_op jit(solution)/shard_map/all_to_all | solution.py:33
  69.4 175.2 %all-gather.14.cloned.1.call-start = ((), (), s32[]{:S(2)}) async-start(), calls=%async_computation.6 | async-start | bytes 3276800 | tf_op jit(solution)/shard_map/all_gather | solution.py:36
  69.6 36.4 %collective-permute-start.1 = (s32[64]{0:T(128)S(1)}, s32[64]{0:T(128)S(1)}, u32[]{:S(2)}, u32[]{:S(2)}) collective-permute-start(s32[64]{0:T(128)S(1)} %get-tuple-element.15), channel_id=1, source_target_pairs={{0,8},{8,0},{16,24},{24,16},{1,9},{9,1},{17,25},{25,17},{2,10},{10... | collective-permute-start | bytes 776 | tf_op jit(solution)/shard_map/ppermute | solution.py:26
  104.2 0.9 copy-start.1
  105.1 156.1 %reduce-scatter.7.cloned.1.call-start = ((), (), s32[]{:S(2)}) async-start(), calls=%async_computation.8 | async-start | bytes 774144
  187.7 25.5 %copy-start.3 = (bf16[32,128,128]{2,1,0:T(8,128)(2,1)S(1)}, bf16[32,128,128]{2,1,0:T(8,128)(2,1)}, u32[]{:S(2)}) copy-start(bf16[32,128,128]{2,1,0:T(8,128)(2,1)} %all-gather.16.cloned.1.call-done) | copy-start | bytes 3145732
  228.3 71.4 %reduce-scatter.5.cloned.1.call-start = ((), (), s32[]{:S(2)}) async-start(), calls=%async_computation.5 | async-start | bytes 2580480 | tf_op jit(solution)/shard_map/reduce_scatter | solution.py:55
Sparse Core Ops, SparseCore 0:
  20.9 40.8 all-gather.15
  63.5 124.1 all-gather.11
  189.5 34.3 all-gather.13
  228.4 32.7 reduce-scatter.6
  264.2 35.4 reduce-scatter.4
where the time goes:
time: 307 us; the launch traced here: 306 us
  waiting for transfers between devices  104 us (34%)
  blocking collectives  96.8 us (32%)
  local copies, waits for them, and re-layouts  56.5 us (18%)
  matrix products  20.3 us (7%)
  between operations  14.6 us (5%)
  starting transfers between devices  11.8 us (4%)
    all_gather x1, waiting for transfers between devices, local(): up = lax.all_gather(cols, 'z', tiled=True).reshape(-1, block_cols)  47.5 us
    reduce_scatter x1, waiting for transfers between devices, local(): merger = lax.psum_scatter(merger, ('y', 'core'), tiled=True)  36.9 us
    all_gather x2, blocking collectives, local(): spots = lax.all_gather(lax.all_gather(spots, 'x'), 'z').reshape(-1)  30.1 us
    all_gather x1, blocking collectives, local(): lax.all_gather(lax.all_gather(audio_places[0], 'x'), 'z').reshape(-1)  25.6 us
    gather x1, local copies, waits for them, and re-layouts, local(): jnp.take(up, audio_spots, axis=0)  25.4 us
    all_to_all x1, blocking collectives, local(): lax.all_to_all(jnp.transpose(upstream.reshape(-1, GRID_COLS, block_cols),...  20.1 us
    gather x1, local copies, waits for them, and re-layouts, local(): jnp.take(up, spots, axis=0)  16 us
    all_gather x1, blocking collectives, local(): lax.all_gather(mel[0], 'x')  13.5 us
  transfers between devices with their start and end apart: 8, of which 4 were waited for; matrix products, arithmetic and copies ran while one was open for 25% of the time, Pallas kernels for 0%

commit v1 on v0

--- a/solution.py
+++ b/solution.py
@@ -19,7 +19,9 @@
     cols = lax.all_to_all(
         jnp.transpose(upstream.reshape(-1, GRID_COLS, block_cols), (1, 0, 2)), "x", 0, 0, tiled=True
     )
-    up = lax.all_gather(cols, "z", tiled=True).reshape(-1, block_cols)
+    up = jnp.concatenate(
+        lax.all_to_all(jnp.stack([cols] * lax.axis_size("z")), "z", 0, 0), axis=0
+    ).reshape(-1, block_cols)
     live_count = video_count[0, 0]
     middle = hidden.shape[0] // 2
     pairs = [(i, i ^ 1) for i in range(lax.axis_size("x"))]

time: 307 us -> 497 us (1.62)
  blocking collectives: 96.8 us -> 317 us
  waiting for transfers between devices: 104 us -> 63.7 us
  local copies, waits for them, and re-layouts: 56.5 us -> 64.1 us
    all_gather x1, blocking collectives: 25.6 us -> 240 us  [local(): lax.all_gather(lax.all_gather(audio_places[0], 'x'), 'z').reshape(-1)]
    all_gather x1 -> x0, waiting for transfers between devices: 47.5 us -> none  [local(): up = lax.all_gather(cols, 'z', tiled=True).reshape(-1, block_cols)]
    all_to_all x1 -> x2, waiting for transfers between devices: 0.01 us -> 12 us  [the longest x1 12 us: local(): lax.all_to_all(jnp.transpose(upstream.reshape(-1, GRID_COLS, block_cols),...]
    all_to_all x1, blocking collectives: 20.1 us -> 27.8 us  [local(): lax.all_to_all(jnp.transpose(rows.reshape(middle, GRID_ROWS, -1), (1, 0,...]
    another operation x0 -> x1, local copies, waits for them, and re-layouts: none -> 6.94 us  [local(): jnp.stack([cols] * lax.axis_size('z'))]
  transfers between devices with their start and end apart: 8 -> 8, of which waited for: 4 -> 4; matrix products, arithmetic and copies ran while one was open for 25% -> 15% of each run, Pallas kernels for 0% -> 0%
where the time goes in v1:
time: 497 us; the launch traced here: 496 us
  blocking collectives  317 us (64%)
  local copies, waits for them, and re-layouts  64.1 us (13%)
  waiting for transfers between devices  63.7 us (13%)
  matrix products  20.3 us (4%)
  starting transfers between devices  15 us (3%)
  between operations  14.6 us (3%)
    all_gather x1, blocking collectives, local(): lax.all_gather(lax.all_gather(audio_places[0], 'x'), 'z').reshape(-1)  240 us
    reduce_scatter x1, waiting for transfers between devices, local(): merger = lax.psum_scatter(merger, ('y', 'core'), tiled=True)  36.9 us
    all_gather x2, blocking collectives, local(): spots = lax.all_gather(lax.all_gather(spots, 'x'), 'z').reshape(-1)  30.1 us
    all_to_all x1, blocking collectives, local(): lax.all_to_all(jnp.transpose(rows.reshape(middle, GRID_ROWS, -1), (1, 0,...  27.8 us
    gather x1, local copies, waits for them, and re-layouts, local(): jnp.take(up, audio_spots, axis=0)  25.5 us
    gather x1, local copies, waits for them, and re-layouts, local(): jnp.take(up, spots, axis=0)  16 us
    dot_general x1, matrix products, local(): lax.dot_general(audio, jnp.take(up, audio_spots, axis=0), contract, prefe...  13.1 us
    all_to_all x1, waiting for transfers between devices, local(): lax.all_to_all(jnp.transpose(upstream.reshape(-1, GRID_COLS, block_cols),...  12 us
  transfers between devices with their start and end apart: 8, of which 4 were waited for; matrix products, arithmetic and copies ran while one was open for 15% of the time, Pallas kernels for 0%

profile of v1, /device:TPU:2, one launch (start us, length us, event | category | flops | bytes accessed | tf_op | source)
XLA Modules:
  0.0 496.4 jit_solution(13168555314223649793)
XLA Ops:
  7.2 0.0 copy-start
  7.2 2.3 slice_bitcast_fusion.1
  9.5 2.3 collective-permute-start
  11.7 2.8 reshape_squeeze.3
  14.5 1.2 copy.18
  15.8 4.3 all-to-all-start.1
  20.8 6.9 %collective-permute-done = bf16[64,5120]{1,0:T(8,128)(2,1)} collective-permute-done((bf16[64,5120]{1,0:T(8,128)(2,1)}, bf16[64,5120]{1,0:T(8,128)(2,1)}, u32[]{:S(2)}, u32[]{:S(2)}) %collective-permute-start) | collective-permute-done | bytes 655392 | tf_op jit(solution)/shard_map/ppermute | solution.py:28
  27.7 1.2 pad_maximum_fusion
  28.9 0.9 gather_fusion
  29.8 0.1 fusion.58
  30.0 12.0 %all-to-all-done.1 = bf16[4,192,896]{2,1,0:T(8,128)(2,1)} async-done(((bf16[4,192,896]{2,1,0:T(8,128)(2,1)}), bf16[4,192,896]{2,1,0:T(8,128)(2,1)}, u32[]{:S(2)}, u32[]{:S(2)}) %all-to-all-start.1) | async-done | bytes 1376288 | tf_op jit(solution)/shard_map/all_to_all | solution.py:19
  41.9 27.8 %all_to_all.15 = bf16[8,64,640]{2,1,0:T(8,128)(2,1)} all-to-all(bf16[8,64,640]{2,1,0:T(8,128)(2,1)S(1)} %fusion.58), channel_id=1, replica_groups=mesh['z'=8,'x'=4,'y'=4,'core'=2] {'z'}, dimensions={0} | all-to-all | bytes 1310720 | tf_op jit(solution)/shard_map/all_to_all | solution.py:35
  69.7 6.9 %stack.2 = bf16[8,4,192,896]{3,2,1,0:T(8,128)(2,1)} broadcast(bf16[4,192,896]{2,1,0:T(8,128)(2,1)} %all-to-all-done.1), dimensions={1,2,3} | broadcast | bytes 12386304 | tf_op jit(solution)/shard_map/stack | solution.py:23
  76.7 5.3 %all-to-all-start.2 = ((bf16[8,4,192,896]{3,2,1,0:T(8,128)(2,1)}), bf16[8,4,192,896]{3,2,1,0:T(8,128)(2,1)}, u32[]{:S(2)}, u32[]{:S(2)}) async-start(bf16[8,4,192,896]{3,2,1,0:T(8,128)(2,1)} %stack.2), calls=%async_computation.2 | async-start | bytes 22020096 | tf_op jit(solution)/shard_map/all_to_all | solution.py:23
  82.0 0.0 all-gather.13.cloned.1.call-start
  82.1 0.0 copy-done.2
  82.1 11.9 %all_gather.39 = bf16[4,128,128]{2,1,0:T(8,128)(2,1)} all-gather(bf16[1,128,128]{2,1,0:T(8,128)(2,1)S(1)} %copy-done.2), channel_id=1, replica_groups=mesh['z'=8,'x'=4,'y'=4,'core'=2] {'x'}, dimensions={0}, use_global_device_ids=true | all-gather | bytes 163840 | tf_op jit(solution)/shard_map/all_gather | solution.py:41
  94.0 0.0 all-gather.13.cloned.1.call-update
  94.0 0.0 all-gather.11.cloned.1.call-start
  94.0 0.0 copy-done.3
  94.0 0.1 slice_bitcast_fusion.3
  94.1 2.7 collective-permute-start.1
  96.8 0.0 copy-done.4
  96.8 6.9 %all-gather.6 = s32[4,1,128]{2,1,0:T(1,128)S(1)} all-gather(s32[1,1,128]{2,1,0:T(1,128)S(1)} %bitcast.52), channel_id=1, replica_groups=mesh['z'=8,'x'=4,'y'=4,'core'=2] {'x'}, dimensions={0}, use_global_device_ids=true | all-gather | bytes 2560 | tf_op jit(solution)/shard_map/all_gather | solution.py:42
  103.7 240.5 %all-gather.7 = s32[8,4,128]{2,1,0:T(4,128)S(1)} all-gather(s32[1,4,128]{2,1,0:T(4,128)S(1)} %bitcast.51), channel_id=5, replica_groups=mesh['z'=8,'x'=4,'y'=4,'core'=2] {'z'}, dimensions={0}, use_global_device_ids=true | all-gather | bytes 18432 | tf_op jit(solution)/shard_map/all_gather | solution.py:42
  344.2 0.0 all-gather.11.cloned.1.call-update
  344.2 0.0 reduce-scatter.7.cloned.1.call-start
  344.3 0.8 dynamic_slice.7
  345.1 0.0 collective-permute-done.1
  345.1 0.1 pad_add_fusion
  345.2 0.8 gather_fusion.1
  346.0 8.7 %all-gather.4 = s32[4,1,64]{2,1,0:T(1,128)S(1)} all-gather(s32[1,1,64]{2,1,0:T(1,128)S(1)} %fusion.62), channel_id=1, replica_groups=mesh['z'=8,'x'=4,'y'=4,'core'=2] {'x'}, dimensions={0}, use_global_device_ids=true | all-gather | bytes 1280 | tf_op jit(solution)/shard_map/all_gather | solution.py:40
  354.7 21.3 %all-gather.5 = s32[8,4,64]{2,1,0:T(4,128)S(1)} all-gather(s32[1,4,64]{2,1,0:T(4,128)S(1)} %bitcast.50), channel_id=3, replica_groups=mesh['z'=8,'x'=4,'y'=4,'core'=2] {'z'}, dimensions={0}, use_global_device_ids=true | all-gather | bytes 9216 | tf_op jit(solution)/shard_map/all_gather | solution.py:40
  376.1 0.1 reshape.195
  376.1 3.1 pad_slice_fusion.1
  379.3 0.0 all-to-all-done.2
  379.3 25.5 %gather_fusion.3 = bf16[4096,896]{1,0:T(8,128)(2,1)} fusion(bf16[6144,896]{1,0:T(8,128)(2,1)} %bitcast.12, s32[4096]{0:T(1024)S(1)} %broadcast_clamp_fusion), kind=kCustom, calls=%fused_computation.3 | custom fusion | bytes 14696448 | tf_op jit(solution)/shard_map/jit(_take)/gather | solution.py:55
  404.7 13.1 %fusion = f32[160,896]{1,0:T(8,128)} fusion(bf16[4096,896]{1,0:T(8,128)(2,1)} %gather_fusion.3, pred[4096]{0:T(1024)(128)(4,1)S(1)} %compare_and_fusion, bf16[4096,128]{1,0:T(8,128)(2,1)} %get-tuple-element.11, bf16[4096,128]{1,0:T(8,128)(2,1)S(1)} %bitcast.45, bf16[4096,128]{1,0:T(8,128)(2,1)S(1)} %get-tuple-element.10, f32[160]{0:T(256)S(1)} %dynamic_slice.7, ...), kind=kOutput, calls=%fused_computation.4 | convolution fusion | flops 1734082560 | bytes 11260932 | tf_op jit(solution)/shard_map/dot_general | solution.py:54
  417.9 2.0 reshape.199
  419.8 0.0 reduce-scatter.7.cloned.1.call-update
  419.9 0.3 reduce-scatter.5.cloned.1.call-start
  420.1 0.1 reshape.194
  420.2 16.0 %gather_fusion.2 = bf16[2048,896]{1,0:T(8,128)(2,1)} fusion(bf16[6144,896]{1,0:T(8,128)(2,1)} %bitcast.12, s32[2048]{0:T(1024)S(1)} %broadcast_clamp_fusion.1), kind=kCustom, calls=%fused_computation.2 | custom fusion | bytes 7348224 | tf_op jit(solution)/shard_map/jit(_take)/gather | solution.py:52
  436.3 7.2 %fusion.4 = f32[640,896]{1,0:T(8,128)} fusion(bf16[2048,640]{1,0:T(8,128)(2,1)} %bitcast.53, bf16[2048,896]{1,0:T(8,128)(2,1)} %gather_fusion.2, pred[2048]{0:T(1024)(128)(4,1)S(1)} %compare_and_fusion.1), kind=kOutput, calls=%fused_computation.10 | convolution fusion | flops 2350645248 | bytes 8587264 | tf_op jit(solution)/shard_map/dot_general | solution.py:51
  443.5 0.0 reduce-scatter.5.cloned.1.call-update
  443.5 7.9 %reduce-scatter.7.cloned.1.call-done = f32[1,20,896]{2,1,0:T(8,128)} async-done(((f32[8,20,896]{2,1,0:T(8,128)}), f32[1,20,896]{2,1,0:T(8,128)}) %reduce-scatter.7.cloned.1.call-update) | async-done | bytes 71696
  451.4 1.6 copy.19
  453.0 36.9 %reduce-scatter.5.cloned.1.call-done = f32[80,896]{1,0:T(8,128)} async-done(((f32[640,896]{1,0:T(8,128)}), f32[80,896]{1,0:T(8,128)}) %reduce-scatter.5.cloned.1.call-update) | async-done | bytes 286736 | tf_op jit(solution)/shard_map/reduce_scatter | solution.py:57
  (18 shorter events, 0.1 us)
Async XLA Ops:
  7.2 397.6 %copy-start = (bf16[384,1280]{1,0:T(8,128)(2,1)S(1)}, bf16[384,1280]{1,0:T(8,128)(2,1)}, u32[]{:S(2)}) copy-start(bf16[384,1280]{1,0:T(8,128)(2,1)} %param.9) | copy-start | bytes 2949124
  9.5 18.2 %collective-permute-start = (bf16[64,5120]{1,0:T(8,128)(2,1)}, bf16[64,5120]{1,0:T(8,128)(2,1)}, u32[]{:S(2)}, u32[]{:S(2)}) collective-permute-start(bf16[64,5120]{1,0:T(8,128)(2,1)} %get-tuple-element.9), channel_id=1, source_target_pairs={{0,8},{8,0},{16,24},{24,16},{1,9},{9,1},{17,25},{25,17},{2,10},{10... | collective-permute-start | bytes 1966088 | tf_op jit(solution)/shard_map/ppermute | solution.py:28
  15.8 26.2 %all-to-all-start.1 = ((bf16[4,192,896]{2,1,0:T(8,128)(2,1)}), bf16[4,192,896]{2,1,0:T(8,128)(2,1)}, u32[]{:S(2)}, u32[]{:S(2)}) async-start(bf16[4,192,896]{2,1,0:T(8,128)(2,1)} %copy.18), calls=%async_computation.1 | async-start | bytes 2752512 | tf_op jit(solution)/shard_map/all_to_all | solution.py:19
  76.7 5.4 %copy-start.2 = (bf16[1,128,128]{2,1,0:T(8,128)(2,1)S(1)}, bf16[1,128,128]{2,1,0:T(8,128)(2,1)}, u32[]{:S(2)}) copy-start(bf16[1,128,128]{2,1,0:T(8,128)(2,1)} %param.8) | copy-start | bytes 98308
  76.7 17.4 %copy-start.3 = (s32[1,128]{1,0:T(1,128)S(1)}, s32[1,128]{1,0:T(1,128)}, u32[]{:S(2)}) copy-start(s32[1,128]{1,0:T(1,128)} %param.13) | copy-start | bytes 1540
  76.7 20.1 %copy-start.4 = (s32[1,128]{1,0:T(1,128)S(1)}, s32[1,128]{1,0:T(1,128)}, u32[]{:S(2)}) copy-start(s32[1,128]{1,0:T(1,128)} %param.14) | copy-start | bytes 1540
  76.7 302.6 %all-to-all-start.2 = ((bf16[8,4,192,896]{3,2,1,0:T(8,128)(2,1)}), bf16[8,4,192,896]{3,2,1,0:T(8,128)(2,1)}, u32[]{:S(2)}, u32[]{:S(2)}) async-start(bf16[8,4,192,896]{3,2,1,0:T(8,128)(2,1)} %stack.2), calls=%async_computation.2 | async-start | bytes 22020096 | tf_op jit(solution)/shard_map/all_to_all | solution.py:23
  82.0 294.1 %all-gather.13.cloned.1.call-start = ((), (), s32[]{:S(2)}) async-start(), calls=%async_computation.7 | async-start | bytes 1179648 | tf_op jit(solution)/shard_map/all_gather | solution.py:41
  94.0 342.3 %all-gather.11.cloned.1.call-start = ((), (), s32[]{:S(2)}) async-start(), calls=%async_computation.6 | async-start | bytes 3276800 | tf_op jit(solution)/shard_map/all_gather | solution.py:38
  94.1 251.0 %collective-permute-start.1 = (s32[64]{0:T(128)S(1)}, s32[64]{0:T(128)S(1)}, u32[]{:S(2)}, u32[]{:S(2)}) collective-permute-start(s32[64]{0:T(128)S(1)} %get-tuple-element.13), channel_id=1, source_target_pairs={{0,8},{8,0},{16,24},{24,16},{1,9},{9,1},{17,25},{25,17},{2,10},{10... | collective-permute-start | bytes 776 | tf_op jit(solution)/shard_map/ppermute | solution.py:28
  344.2 107.1 %reduce-scatter.7.cloned.1.call-start = ((), (), s32[]{:S(2)}) async-start(), calls=%async_computation.8 | async-start | bytes 774144
  379.3 25.5 %copy-start.1 = (bf16[32,128,128]{2,1,0:T(8,128)(2,1)S(1)}, bf16[32,128,128]{2,1,0:T(8,128)(2,1)}, u32[]{:S(2)}) copy-start(bf16[32,128,128]{2,1,0:T(8,128)(2,1)} %all-gather.13.cloned.1.call-done) | copy-start | bytes 3145732
  419.9 70.0 %reduce-scatter.5.cloned.1.call-start = ((), (), s32[]{:S(2)}) async-start(), calls=%async_computation.5 | async-start | bytes 2580480 | tf_op jit(solution)/shard_map/reduce_scatter | solution.py:57
Sparse Core Ops, SparseCore 0:
  94.1 57.3 all-gather.12
  344.3 35.3 all-gather.10
  420.0 31.3 reduce-scatter.6
  454.4 35.4 reduce-scatter.4
